TPU v7x, 32 devices: a whole 2x2x4 slice. The times are simulated.
32 devices in a mesh: dp: 4 (over y, x), expert: 8 (over z, core).
Axes of the slice: x: 2, y: 2, z: 4, core: 2. Of those that a mesh axis runs over, the one named last changes fastest.
Arguments:
- tokens: bfloat16 [6144, 2048], P(('dp', 'expert')), may hold values from -6 to 6
- modality: int32 [6144], P(('dp', 'expert')), may hold values from 0 to 1, as said below
- local_expert: int32 [6144], P(('dp', 'expert')), may hold values from 0 to 1, as said below
- combine_weight: float32 [6144], P(('dp', 'expert')), may hold values from 0.3 to 1
- norm_gain: float32 [2, 2048], replicated, may hold values from 0.1 to 1.9
- gate_weight: bfloat16 [2048, 16384], P('dp', 'expert'), may hold values from -0.125 to 0.125
- up_weight: bfloat16 [2048, 16384], P('dp', 'expert'), may hold values from -0.125 to 0.125
- down_weight: bfloat16 [16384, 2048], P('expert', 'dp'), may hold values from -0.09375 to 0.09375
Outputs:
- mixed: bfloat16 [6144, 2048], P(('dp', 'expert'))
Inputs may be any that keep to these rules, and one draw needn't show every extreme that they name: Expert e = modality * 2 + local_expert. Among the 192 rows of each device (aligned blocks in order) no expert is chosen by more than 72 rows, and on every device one expert is chosen by exactly 72. `local_expert`: drawn together with modality under the bound stated there.
All inputs are finite; a program needn't handle non-finite values.
Results may differ from a plain program's by a relative error of at most 0.005.
Values may be sent and summed in bfloat16 or wider, within the bound.
A program may use at most 128 MiB of HBM per device.

v0:
```python
import jax
import jax.numpy as jnp
from jax import lax
from jax.sharding import PartitionSpec as P

EXP_MOD = 2
EXPERTS = 4
CAP = 72


def partner(value, axis, apart):
    return lax.ppermute(value, axis, [(i, i ^ 1 << apart) for i in range(lax.axis_size(axis))])


def body(
    tokens, modality, local_expert, combine_weight, norm_gain, gate_weight, up_weight, down_weight
):
    width = tokens.shape[1]
    resid = tokens.astype(jnp.float32)
    root_mean = jnp.sqrt(jnp.mean(resid * resid, axis=1, keepdims=True) + 1e-05)
    row_gain = jnp.where(modality[:, None] == 0, norm_gain[0][None, :], norm_gain[1][None, :])
    normed = (resid / root_mean * row_gain).astype(jnp.bfloat16)
    route = modality * EXP_MOD + local_expert
    onehot = (route[:, None] == jnp.arange(EXPERTS, dtype=jnp.int32)[None, :]).astype(jnp.int32)
    row_rank = jnp.sum((jnp.cumsum(onehot, axis=0) - 1) * onehot, axis=1)
    position = route * CAP + row_rank
    placing = position[:, None] == jnp.arange(EXPERTS * CAP, dtype=jnp.int32)[None, :]
    buffer = jnp.einsum(
        "ts,td->sd", placing.astype(jnp.bfloat16), normed, preferred_element_type=jnp.float32
    ).astype(jnp.bfloat16)
    devices = lax.axis_size("expert")
    group = devices // EXPERTS
    piece_rows = CAP // group
    bit_count = group.bit_length() - 1
    place = lax.axis_index("expert") % group
    sent = lax.all_to_all(
        buffer.reshape(devices, piece_rows, width),
        "expert",
        split_axis=0,
        concat_axis=0,
        tiled=True,
    )
    held = sent.reshape(1, devices * piece_rows, width)
    for bit in range(bit_count):
        other = partner(held, "expert", bit)
        upper = place // (1 << bit) % 2 == 1
        held = jnp.where(
            upper, jnp.concatenate([other, held], axis=0), jnp.concatenate([held, other], axis=0)
        )
    arrival = held.reshape(group * devices * piece_rows, width)
    gate_full, up_full = (
        lax.all_gather(gate_weight, "dp", axis=0, tiled=True),
        lax.all_gather(up_weight, "dp", axis=0, tiled=True),
    )
    gate_acts = jnp.dot(arrival, gate_full, preferred_element_type=jnp.float32)
    up_acts = jnp.dot(arrival, up_full, preferred_element_type=jnp.float32)
    hidden = (jax.nn.silu(gate_acts) * up_acts).astype(jnp.bfloat16)
    partial_out = jnp.dot(
        hidden,
        lax.all_gather(down_weight, "dp", axis=1, tiled=True),
        preferred_element_type=jnp.float32,
    ).astype(jnp.bfloat16)
    totals = partial_out.astype(jnp.float32).reshape(group, devices * piece_rows, width)
    for bit in reversed(range(bit_count)):
        halves = totals.reshape(2, totals.shape[0] // 2, devices * piece_rows, width)
        upper = place // (1 << bit) % 2 == 1
        keeping = jnp.where(upper, halves[1], halves[0])
        giving = jnp.where(upper, halves[0], halves[1])
        totals = keeping + partner(giving.astype(jnp.bfloat16), "expert", bit).astype(giving.dtype)
    summed = (
        lax.all_to_all(
            totals.reshape(devices, piece_rows, width).astype(jnp.bfloat16),
            "expert",
            split_axis=0,
            concat_axis=0,
            tiled=True,
        )
        .astype(jnp.float32)
        .reshape(EXPERTS * CAP, width)
    )
    moe_out = jnp.dot(placing.astype(jnp.float32), summed, precision=lax.Precision.HIGHEST)
    return (resid + combine_weight[:, None] * moe_out).astype(jnp.bfloat16)


def solution(mesh):
    in_specs = (
        P(("dp", "expert"), None),
        P(("dp", "expert")),
        P(("dp", "expert")),
        P(("dp", "expert")),
        P(),
        P("dp", "expert"),
        P("dp", "expert"),
        P("expert", "dp"),
    )
    out_specs = P(("dp", "expert"), None)
    return jax.shard_map(body, mesh=mesh, in_specs=in_specs, out_specs=out_specs, check_vma=False)
```

profile of v0, /device:TPU:0, one launch (start us, length us, event | category | flops | bytes accessed | tf_op | source)
XLA Modules:
  0.0 351.7 jit_solution(14837671481226897695)
XLA Ops:
  6.5 0.0 all-gather.4.cloned.1.call-start
  6.5 0.7 all-gather.4.cloned.1.call-update
  7.3 0.0 copy-start.4
  7.3 0.0 copy-start.5
  7.3 0.0 copy-start
  7.3 0.0 copy-start.2
  7.3 0.0 all-gather.6.cloned.1.call-start
  7.3 0.7 all-gather.6.cloned.1.call-update
  8.0 0.0 all-gather.8.cloned.1.call-start
  8.1 0.7 all-gather.8.cloned.1.call-update
  8.8 0.0 copy-done.4
  8.8 0.0 copy-done.5
  8.9 1.2 reduce-window.6
  10.1 0.1 slice.32
  10.2 0.1 copy.11
  10.3 0.1 copy.12
  10.4 0.1 add_bitcast_fusion
  10.5 0.0 copy-done
  10.5 0.2 fusion.4
  10.8 0.0 copy-done.2
  10.8 0.6 convolution_convert_fusion.1
  11.5 0.3 reshape.49
  11.8 38.3 %all_to_all.10 = bf16[8,36,2048]{2,1,0:T(8,128)(2,1)S(1)} all-to-all(bf16[8,36,2048]{2,1,0:T(8,128)(2,1)S(1)} %reshape.49), channel_id=1, replica_groups=mesh['dp'=4,'expert'=8] {'expert'}, dimensions={0} | all-to-all | bytes 2359296 | tf_op jit(solution)/shard_map/all_to_all | solution.py:36
  50.1 0.3 reshape.50
  50.4 0.1 collective-permute-start
  50.5 2.8 collective-permute-done
  53.3 1.7 maximum_select_fusion
  55.0 44.5 %all-gather.4.cloned.1.call-done = bf16[2048,2048]{1,0:T(8,128)(2,1)} async-done(((bf16[512,2048]{1,0:T(8,128)(2,1)}), bf16[2048,2048]{1,0:T(8,128)(2,1)}) %all-gather.4.cloned.1.call-update) | async-done | bytes 8388624 | tf_op jit(solution)/shard_map/all_gather | solution.py:52
  99.5 0.0 copy-start.1
  99.6 10.6 %fusion.18 = f32[576,2048]{1,0:T(8,128)} fusion(bf16[576,2048]{1,0:T(8,128)(2,1)} %bitcast.33, bf16[2048,2048]{1,0:T(8,128)(2,1)} %all-gather.4.cloned.1.call-done), kind=kOutput, calls=%fused_computation.37 | convolution fusion | flops 4831838208 | bytes 15466496 | tf_op jit(solution)/shard_map/dot_general | solution.py:55
  110.2 78.9 %all-gather.6.cloned.1.call-done = bf16[2048,2048]{1,0:T(8,128)(2,1)} async-done(((bf16[512,2048]{1,0:T(8,128)(2,1)}), bf16[2048,2048]{1,0:T(8,128)(2,1)}) %all-gather.6.cloned.1.call-update) | async-done | bytes 8388624 | tf_op jit(solution)/shard_map/all_gather | solution.py:53
  189.0 89.3 %all-gather.8.cloned.1.call-done = bf16[2048,2048]{1,0:T(8,128)(2,1)} async-done(((bf16[2048,512]{1,0:T(8,128)(2,1)}), bf16[2048,2048]{1,0:T(8,128)(2,1)}) %all-gather.8.cloned.1.call-update) | async-done | bytes 8388624 | tf_op jit(solution)/shard_map/all_gather | solution.py:60
  278.4 0.0 copy-done.1
  278.4 19.6 %fusion = f32[576,2048]{1,0:T(8,128)} fusion(bf16[2048,2048]{1,0:T(8,128)(2,1)} %all-gather.8.cloned.1.call-done, f32[576,2048]{1,0:T(8,128)} %fusion.18, bf16[576,2048]{1,0:T(8,128)(2,1)S(1)} %bitcast.34, bf16[2048,2048]{1,0:T(8,128)(2,1)} %all-gather.6.cloned.1.call-done), kind=kOutput, calls=%fused_computation.2 | convolution fusion | flops 9673113600 | bytes 28573696 | tf_op jit(solution)/shard_map/dot_general | solution.py:58
  298.0 2.6 fusion.7
  300.6 0.1 collective-permute-start.1
  300.6 2.8 collective-permute-done.1
  303.5 3.0 fusion.3
  306.4 0.3 convert_element_type.51
  306.7 0.0 copy-start.3
  306.7 36.6 %all_to_all.11 = bf16[8,36,2048]{2,1,0:T(8,128)(2,1)S(1)} all-to-all(bf16[8,36,2048]{2,1,0:T(8,128)(2,1)S(1)} %convert_element_type.51), channel_id=1, replica_groups=mesh['dp'=4,'expert'=8] {'expert'}, dimensions={0} | all-to-all | bytes 2359296 | tf_op jit(solution)/shard_map/all_to_all | solution.py:71
  343.4 0.3 reshape.51
  343.6 0.0 copy-done.3
  343.6 1.5 fusion.2
  (12 shorter events, 0.1 us)
Async XLA Ops:
  6.5 93.0 %all-gather.4.cloned.1.call-start = ((), (), s32[]{:S(2)}) async-start(), calls=%async_computation.2 | async-start | bytes 10485760 | tf_op jit(solution)/shard_map/all_gather | solution.py:52
  7.3 1.5 copy-start.4
  7.3 1.5 copy-start.5
  7.3 3.2 copy-start
  7.3 3.5 copy-start.2
  7.3 181.7 %all-gather.6.cloned.1.call-start = ((), (), s32[]{:S(2)}) async-start(), calls=%async_computation.3 | async-start | bytes 10485760 | tf_op jit(solution)/shard_map/all_gather | solution.py:53
  8.0 270.3 %all-gather.8.cloned.1.call-start = ((), (), s32[]{:S(2)}) async-start(), calls=%async_computation.4 | async-start | bytes 10485760 | tf_op jit(solution)/shard_map/all_gather | solution.py:60
  50.4 2.9 collective-permute-start
  99.5 178.8 %copy-start.1 = (bf16[2,288,2048]{2,1,0:T(8,128)(2,1)S(1)}, bf16[2,288,2048]{2,1,0:T(8,128)(2,1)}, u32[]{:S(2)}) copy-start(bf16[2,288,2048]{2,1,0:T(8,128)(2,1)} %maximum_select_fusion) | copy-start | bytes 7077892
  300.6 2.9 collective-permute-start.1
  306.7 36.9 %copy-start.3 = (f32[192]{0:T(256)S(1)}, f32[192]{0:T(256)}, u32[]{:S(2)}) copy-start(f32[192]{0:T(256)} %param.11) | copy-start | bytes 2308
Sparse Core Ops, SparseCore 0:
  9.2 90.3 all-gather.3
  101.4 87.5 all-gather.5
  190.9 87.4 all-gather.7
where the time goes:
time: 352 us
  waiting for transfers between devices  220 us (62%)
  blocking collectives  74.9 us (21%)
  matrix products  32.4 us (9%)
  between operations  13.3 us (4%)
  other arithmetic  8.92 us (3%)
    all_gather x1, waiting for transfers between devices, body(): lax.all_gather(down_weight, 'dp', axis=1, tiled=True)  89.3 us
    all_gather x1, waiting for transfers between devices, body(): lax.all_gather(up_weight, 'dp', axis=0, tiled=True)  78.9 us
    all_gather x1, waiting for transfers between devices, body(): lax.all_gather(gate_weight, 'dp', axis=0, tiled=True)  44.5 us
    all_to_all x1, blocking collectives, body(): lax.all_to_all(buffer.reshape(devices, piece_rows, width), 'expert', spli...  38.3 us
    all_to_all x1, blocking collectives, body(): lax.all_to_all(totals.reshape(devices, piece_rows, width).astype(jnp.bflo...  36.6 us
    dot_general x1, matrix products, body(): jnp.dot(hidden, lax.all_gather(down_weight, 'dp', axis=1, tiled=True), pr...  19.6 us
    dot_general x1, matrix products, body(): gate_acts = jnp.dot(arrival, gate_full, preferred_element_type=jnp.float32)  10.6 us
  transfers between devices with their start and end apart: 5, of which 5 were waited for; matrix products, arithmetic and copies ran while one was open for 4% of the time, Pallas kernels for 0%

commit v1 on v0

v1 whole, which is shorter than its diff:
```python
import functools

import jax
import jax.numpy as jnp
from jax import lax
from jax.experimental import pallas as pl
from jax.experimental.pallas import tpu as pltpu
from jax.sharding import PartitionSpec as P

EXP_MOD = 2
EXPERTS = 4
CAP = 72
SLOTS = -(-CAP // 16) * 16
ROWS = EXPERTS * CAP
VMEM_LIMIT = 60 << 20


def tiles(total, width, step):
    def one(i, carry):
        step(pl.multiple_of(i * width, width))
        return carry

    lax.fori_loop(0, total // width, one, 0)


def kernel(
    dp, share, group,
    buf, gate, up, down,
    out,
    zin, arr, wg, wu, wd, hid, part, core_in, dp_in, wide, zout,
    z_s, z_r, w_s, w_r, w_l, b_s, b_r, f_s, f_r, c_s, c_r, d_s, d_r, o_s, o_r, l_s,
):
    d = lax.axis_index("dp")
    p = lax.axis_index("expert")
    e, g = p // group, lax.rem(p, group)
    base, r = d // share * share, lax.rem(d, share)
    deep, cut, width = gate.shape[0], down.shape[1], buf.shape[-1]
    units = wg.shape[1]

    def dp_peer(k):
        return (lax.rem(d + k, dp), p)

    def share_peer(k):
        return (base + lax.rem(r + k, share), p)

    def z_peer(k):
        return (d, lax.rem(e + k, EXPERTS) * group + g)

    def core_peer(m):
        return (d, e * group + lax.rem(g + m, group))

    def send(src, dst, s, q, to):
        return pltpu.make_async_remote_copy(
            src_ref=src, dst_ref=dst, send_sem=s, recv_sem=q,
            device_id=to, device_id_type=pl.DeviceIdType.MESH,
        )

    peers = (
        [dp_peer(k) for k in range(1, dp)]
        + [z_peer(k) for k in range(1, EXPERTS)]
        + [core_peer(m) for m in range(1, group)]
    )
    barrier = pltpu.get_barrier_semaphore()
    for peer in peers:
        pl.semaphore_signal(barrier, inc=1, device_id=peer, device_id_type=pl.DeviceIdType.MESH)
    pl.semaphore_wait(barrier, len(peers))

    sent = []

    def go(copy):
        copy.start()
        sent.append(copy)
        return copy

    z_copies = [
        go(send(buf.at[k], zin.at[k], z_s.at[k], z_r.at[k], z_peer(k))) for k in range(1, EXPERTS)
    ]
    own_rows = pltpu.make_async_copy(buf.at[0], zin.at[0], l_s.at[0])
    own_rows.start()

    my_units = pl.ds(pl.multiple_of(r * units, units), units)
    my_deep = pl.ds(pl.multiple_of(d * deep, deep), deep)
    my_cut = pl.ds(pl.multiple_of(d * cut, cut), cut)
    own_w = [
        pltpu.make_async_copy(gate.at[:, my_units], wg.at[my_deep, :], w_l.at[0]),
        pltpu.make_async_copy(up.at[:, my_units], wu.at[my_deep, :], w_l.at[1]),
        pltpu.make_async_copy(down.at[my_units, :], wd.at[:, my_cut], w_l.at[2]),
    ]
    for copy in own_w:
        copy.start()

    def weight_copies(which):
        made = []
        for k in range(1, dp):
            theirs = lax.rem(lax.rem(d + k, dp), share)
            units_k = pl.ds(pl.multiple_of(theirs * units, units), units)
            if which == 2:
                src, dst = down.at[units_k, :], wd.at[:, my_cut]
            else:
                src, dst = (gate, up)[which].at[:, units_k], (wg, wu)[which].at[my_deep, :]
            made.append(go(send(src, dst, w_s.at[which, k], w_r.at[which, k], dp_peer(k))))
        return made

    gate_copies = weight_copies(0)
    up_copies = weight_copies(1)

    own_rows.wait()
    for copy in z_copies:
        copy.wait_recv()
    for i in range(EXPERTS):

        def widen(at, i=i):
            wide[i * CAP : (i + 1) * CAP, pl.ds(at, 256)] = zin[i, :, pl.ds(at, 256)].astype(
                jnp.float32
            )[:CAP]

        tiles(width, 256, widen)

    def narrow(at):
        arr[0, 0, :, pl.ds(at, 256)] = wide[:, pl.ds(at, 256)].astype(jnp.bfloat16)

    tiles(width, 256, narrow)

    rows_in = {}
    for k in range(1, share):
        rows_in[k] = go(send(arr.at[0, 0], arr.at[k, 0], b_s.at[k], b_r.at[k], share_peer(k)))
    core_rows = {}

    def forward(k):
        for m in range(1, group):
            core_rows[k, m] = go(
                send(arr.at[k, 0], arr.at[k, m], f_s.at[k, m], f_r.at[k, m], core_peer(m))
            )

    forward(0)
    down_copies = weight_copies(2)
    for k in range(1, share):
        rows_in[k].wait_recv()
        forward(k)

    for copy in (*own_w[:2],):
        copy.wait()
    for copy in (*gate_copies, *up_copies):
        copy.wait_recv()

    core_sums = {}
    dp_sums = {}
    rows = group * ROWS

    def finish(k):
        for m in range(1, group):
            core_sums[k, m].wait_recv()

        def add(at):
            cols = pl.ds(at, 256)
            total = part[k, 0, :, cols].astype(jnp.float32)
            for m in range(1, group):
                total = total + core_in[k, m, :, cols].astype(jnp.float32)
            part[k, 0, :, cols] = total.astype(jnp.bfloat16)

        tiles(width, 256, add)
        if k:
            dp_sums[k] = go(
                send(part.at[k, 0], dp_in.at[k], d_s.at[k], d_r.at[k], share_peer(share - k))
            )

    order = [*range(1, share), 0]
    for n, k in enumerate(order):
        for m in range(1, group):
            core_rows[k, m].wait_recv()

        def first(at, k=k):
            cols = pl.ds(at, 256)
            x = arr[k].reshape(rows, width)
            gated = jnp.dot(x, wg[:, cols], preferred_element_type=jnp.float32)
            lifted = jnp.dot(x, wu[:, cols], preferred_element_type=jnp.float32)
            hid[:, cols] = (gated / (1.0 + jnp.exp(-gated)) * lifted).astype(jnp.bfloat16)

        tiles(units, 256, first)
        if n == 0:
            own_w[2].wait()
            for copy in down_copies:
                copy.wait_recv()

        def second(at, k=k):
            cols = pl.ds(at, 256)
            made = jnp.dot(hid[...], wd[:, cols], preferred_element_type=jnp.float32)
            part[k, :, :, cols] = made.astype(jnp.bfloat16).reshape(group, ROWS, 256)

        tiles(width, 256, second)
        for m in range(1, group):
            core_sums[k, m] = go(
                send(part.at[k, m], core_in.at[k, m], c_s.at[k, m], c_r.at[k, m], core_peer(group - m))
            )
        if n:
            finish(order[n - 1])
    finish(order[-1])

    for k in range(1, share):
        dp_sums[k].wait_recv()

    def gather(at):
        cols = pl.ds(at, 256)
        total = part[0, 0, :, cols].astype(jnp.float32)
        for k in range(1, share):
            total = total + dp_in[k, :, cols].astype(jnp.float32)
        wide[:, cols] = total

    tiles(width, 256, gather)
    home = []
    for i in [*range(1, EXPERTS), 0]:
        to = out if i == 0 else zout

        def split(at, i=i, to=to):
            cols = pl.ds(at, 256)
            full = jnp.concatenate(
                [wide[i * CAP : (i + 1) * CAP, cols], jnp.zeros((SLOTS - CAP, 256), jnp.float32)], 0
            )
            to[i, :, cols] = full.astype(jnp.bfloat16)

        tiles(width, 256, split)
        if i:
            home.append(
                go(send(zout.at[i], out.at[i], o_s.at[i], o_r.at[i], z_peer(EXPERTS - i)))
            )
    for copy in home:
        copy.wait_recv()
    for copy in sent:
        copy.wait_send()


def shared_by(dp, group, width, hidden):
    for share in range(dp, 0, -1):
        if dp % share or hidden % share or hidden // share % 256:
            continue
        block = ROWS * width * 2
        units = hidden // share
        held = (
            block * (share * group * 2 + share * (group - 1) + share + 2)
            + 3 * width * units * 2
            + group * ROWS * units * 2
            + 4 * EXPERTS * SLOTS * width * 2
        )
        if held <= VMEM_LIMIT * 2 // 3:
            return share
    return 1


def experts(buffer, gate, up, down):
    dp, group = lax.axis_size("dp"), lax.axis_size("expert") // EXPERTS
    width, hidden = buffer.shape[-1], gate.shape[1]
    share = shared_by(dp, group, width, hidden)
    units = hidden // share
    bf16, dma = jnp.bfloat16, pltpu.SemaphoreType.DMA
    whole = pl.BlockSpec(memory_space=pltpu.VMEM)
    far = pl.BlockSpec(memory_space=pl.ANY)
    pairs = lambda *shape: [dma(shape), dma(shape)]
    return pl.pallas_call(
        functools.partial(kernel, dp, share, group),
        out_shape=jax.ShapeDtypeStruct(buffer.shape, bf16),
        in_specs=[whole, far, far, far],
        out_specs=whole,
        scratch_shapes=[
            pltpu.VMEM((EXPERTS, SLOTS, width), bf16),
            pltpu.VMEM((share, group, ROWS, width), bf16),
            pltpu.VMEM((width, units), bf16),
            pltpu.VMEM((width, units), bf16),
            pltpu.VMEM((units, width), bf16),
            pltpu.VMEM((group * ROWS, units), bf16),
            pltpu.VMEM((share, group, ROWS, width), bf16),
            pltpu.VMEM((share, group, ROWS, width), bf16),
            pltpu.VMEM((share, ROWS, width), bf16),
            pltpu.VMEM((ROWS, width), jnp.float32),
            pltpu.VMEM((EXPERTS, SLOTS, width), bf16),
            *pairs(EXPERTS),
            *pairs(3, dp),
            dma((3,)),
            *pairs(share),
            *pairs(share, group),
            *pairs(share, group),
            *pairs(share),
            *pairs(EXPERTS),
            dma((1,)),
        ],
        compiler_params=pltpu.CompilerParams(
            collective_id=0, has_side_effects=True, vmem_limit_bytes=VMEM_LIMIT
        ),
        cost_estimate=pl.CostEstimate(
            flops=6 * share * group * ROWS * width * units,
            bytes_accessed=3 * width * hidden * 2,
            transcendentals=share * group * ROWS * units,
        ),
    )(buffer, gate, up, down)


def body(
    tokens, modality, local_expert, combine_weight, norm_gain, gate_weight, up_weight, down_weight
):
    count, width = tokens.shape
    resid = tokens.astype(jnp.float32)
    root_mean = jnp.sqrt(jnp.mean(resid * resid, axis=1, keepdims=True) + 1e-05)
    row_gain = jnp.where(modality[:, None] == 0, norm_gain[0][None, :], norm_gain[1][None, :])
    normed = (resid / root_mean * row_gain).astype(jnp.bfloat16)
    route = modality * EXP_MOD + local_expert
    at = jnp.arange(count, dtype=jnp.int32)
    earlier = (route[:, None] == route[None, :]) & (at[None, :] < at[:, None])
    row_rank = jnp.sum(earlier.astype(jnp.int32), axis=1)
    own = lax.axis_index("expert") // (lax.axis_size("expert") // EXPERTS)
    position = (route - own + EXPERTS) % EXPERTS * SLOTS + row_rank
    placing = (
        position[:, None] == jnp.arange(EXPERTS * SLOTS, dtype=jnp.int32)[None, :]
    ).astype(jnp.bfloat16)
    buffer = jnp.einsum("ts,td->sd", placing, normed, preferred_element_type=jnp.float32)
    buffer = buffer.astype(jnp.bfloat16).reshape(EXPERTS, SLOTS, width)
    summed = experts(buffer, gate_weight, up_weight, down_weight)
    moe_out = jnp.dot(
        placing, summed.reshape(EXPERTS * SLOTS, width), preferred_element_type=jnp.float32
    )
    return (resid + combine_weight[:, None] * moe_out).astype(jnp.bfloat16)


def solution(mesh):
    in_specs = (
        P(("dp", "expert"), None),
        P(("dp", "expert")),
        P(("dp", "expert")),
        P(("dp", "expert")),
        P(),
        P("dp", "expert"),
        P("dp", "expert"),
        P("expert", "dp"),
    )
    out_specs = P(("dp", "expert"), None)
    return jax.shard_map(body, mesh=mesh, in_specs=in_specs, out_specs=out_specs, check_vma=False)
```

time: 352 us -> 249 us (0.71)
  Pallas kernels: 0 us -> 239 us
  waiting for transfers between devices: 220 us -> 0 us
  blocking collectives: 74.9 us -> 0 us
  matrix products: 32.4 us -> 5.71 us
  between operations: 13.3 us -> 0.04 us
  other arithmetic: 8.92 us -> 2.97 us
    pallas_call x0 -> x1, Pallas kernels: none -> 239 us  [experts(): pl.pallas_call(functools.partial(kernel, dp, share, group), out_shape=jax...]
    all_gather x3 -> x0, waiting for transfers between devices: 213 us -> none  [the longest x1 89.3 us: body(): lax.all_gather(down_weight, 'dp', axis=1, tiled=True)]
    all_to_all x2 -> x0, blocking collectives: 74.9 us -> none  [the longest x1 38.3 us: body(): lax.all_to_all(buffer.reshape(devices, piece_rows, width), 'expert', spli...]
    dot_general x4 -> x2, matrix products: 32.4 us -> 5.71 us  [the longest x1 2.88 us: body(): jnp.einsum('ts,td->sd', placing, normed, preferred_element_type=jnp.float32)]
    ppermute x2 -> x0, waiting for transfers between devices: 5.64 us -> none  [partner(): lax.ppermute(value, axis, [(i, i ^ 1 << apart) for i in range(lax.axis_si...]
    convert_element_type x2 -> x0, other arithmetic: 5.55 us -> none  [the longest x1 2.97 us: body(): totals.reshape(devices, piece_rows, width).astype(jnp.bfloat16)]
  transfers between devices with their start and end apart: 5 -> 0, of which waited for: 5 -> 0; matrix products, arithmetic and copies ran while one was open for 4% -> 0% of each run, Pallas kernels for 0% -> 0%
where the time goes in v1:
time: 249 us
  Pallas kernels  239 us (96%)
  matrix products  5.71 us (2%)
  other arithmetic  2.97 us (1%)
    pallas_call x1, Pallas kernels, experts(): pl.pallas_call(functools.partial(kernel, dp, share, group), out_shape=jax...  239 us

profile of v1, /device:TPU:0, one launch (start us, length us, event | category | flops | bytes accessed | tf_op | source)
XLA Modules:
  0.0 248.9 jit_solution(3257447136815290419)
XLA Ops:
  0.0 0.7 broadcast_compare_fusion
  0.7 0.7 multiply_add_fusion
  1.4 0.2 convert_reduce_fusion
  1.6 1.4 fusion.2
  3.0 0.8 fusion.16
  3.8 2.9 %convolution_convert_fusion = bf16[320,2048]{1,0:T(8,128)(2,1)} fusion(bf16[192,2048]{1,0:T(8,128)(2,1)} %param.8, f32[2048]{0:T(1024)S(1)} %bitcast.7, f32[2048]{0:T(1024)S(1)} %bitcast.6, f32[192]{0:T(256)S(1)} %add_sqrt_fusion, pred[192]{0:T(512)(128)(4,1)S(1)} %broadcast_compare_fusion, s32[192]{0:T(256)S(1)} %fusion.14), kind=kOutput, calls=%fused_computation | convolution fusion | flops 254341120 | bytes 2115264 | tf_op jit(solution)/shard_map/ts,td->sd/dot_general | solution.py:313
  6.7 0.0 copy-start
  6.7 0.0 copy-start.1
  6.7 239.4 %shard_map.82 = bf16[4,80,2048]{2,1,0:T(8,128)(2,1)} custom-call(bf16[4,80,2048]{2,1,0:T(8,128)(2,1)} %bitcast.8, bf16[512,2048]{1,0:T(8,128)(2,1)} %gate.1, bf16[512,2048]{1,0:T(8,128)(2,1)} %up.1, bf16[2048,512]{1,0:T(8,128)(2,1)} %down.1), custom_call_target="tpu_custom_call" | custom-call | flops 14495514624 | bytes 25165824 | tf_op jit(solution)/shard_map/pallas_call | solution.py:258
  246.1 0.0 copy-done
  246.1 0.0 copy-done.1
  246.1 2.8 %fusion.1 = bf16[192,2048]{1,0:T(8,128)(2,1)} fusion(bf16[320,2048]{1,0:T(8,128)(2,1)} %bitcast.5, bf16[192,2048]{1,0:T(8,128)(2,1)S(1)} %copy-done, f32[192]{0:T(256)S(1)} %copy-done.1, s32[192]{0:T(256)S(1)} %fusion.14), kind=kOutput, calls=%fused_computation.3 | convolution fusion | flops 253292544 | bytes 2885120 | tf_op jit(solution)/shard_map/dot_general | solution.py:316
  (2 shorter events, 0.0 us)
Async XLA Ops:
  6.7 239.4 %copy-start = (bf16[192,2048]{1,0:T(8,128)(2,1)S(1)}, bf16[192,2048]{1,0:T(8,128)(2,1)}, u32[]{:S(2)}) copy-start(bf16[192,2048]{1,0:T(8,128)(2,1)} %param.8) | copy-start | bytes 2359300
  6.7 239.4 %copy-start.1 = (f32[192]{0:T(256)S(1)}, f32[192]{0:T(256)}, u32[]{:S(2)}) copy-start(f32[192]{0:T(256)} %param.11) | copy-start | bytes 2308

commit v2 on v1

--- a/solution.py
+++ b/solution.py
@@ -12,7 +12,21 @@
 CAP = 72
 SLOTS = -(-CAP // 16) * 16
 ROWS = EXPERTS * CAP
+PIECES = 4
 VMEM_LIMIT = 60 << 20
+
+
+def partner(i, k, n):
+    if n & (n - 1):
+        return lax.rem(i + k, n)
+    for bit in range(n.bit_length()):
+        if k >> bit & 1:
+            i = i + (1 - 2 * (i // (1 << bit) % 2)) * (1 << bit)
+    return i
+
+
+def back(k, n):
+    return n - k if n & (n - 1) else k
 
 
 def tiles(total, width, step):
@@ -27,8 +41,8 @@
     dp, share, group,
     buf, gate, up, down,
     out,
-    zin, arr, wg, wu, wd, hid, part, core_in, dp_in, wide, zout,
-    z_s, z_r, w_s, w_r, w_l, b_s, b_r, f_s, f_r, c_s, c_r, d_s, d_r, o_s, o_r, l_s,
+    zin, arr, wg, wu, wd, hid, part, core_in, dp_in, relay_in, wide, zout,
+    z_s, z_r, w_s, w_r, w_l, b_s, b_r, f_s, f_r, c_s, c_r, d_s, d_r, r_s, r_r, o_s, o_r, l_s,
 ):
     d = lax.axis_index("dp")
     p = lax.axis_index("expert")
@@ -36,12 +50,15 @@
     base, r = d // share * share, lax.rem(d, share)
     deep, cut, width = gate.shape[0], down.shape[1], buf.shape[-1]
     units = wg.shape[1]
+    half, piece = ROWS // 2, width // PIECES
+    relay = share == 4
+    low, high = pl.ds(0, half), pl.ds(half, half)
 
     def dp_peer(k):
-        return (lax.rem(d + k, dp), p)
+        return (partner(d, k, dp), p)
 
     def share_peer(k):
-        return (base + lax.rem(r + k, share), p)
+        return (base + partner(r, k, share), p)
 
     def z_peer(k):
         return (d, lax.rem(e + k, EXPERTS) * group + g)
@@ -92,7 +109,7 @@
     def weight_copies(which):
         made = []
         for k in range(1, dp):
-            theirs = lax.rem(lax.rem(d + k, dp), share)
+            theirs = lax.rem(partner(d, k, dp), share)
             units_k = pl.ds(pl.multiple_of(theirs * units, units), units)
             if which == 2:
                 src, dst = down.at[units_k, :], wd.at[:, my_cut]
@@ -123,7 +140,10 @@
 
     rows_in = {}
     for k in range(1, share):
-        rows_in[k] = go(send(arr.at[0, 0], arr.at[k, 0], b_s.at[k], b_r.at[k], share_peer(k)))
+        if not (relay and k == 3):
+            rows_in[k] = [
+                go(send(arr.at[0, 0], arr.at[k, 0], b_s.at[k], b_r.at[k], share_peer(k)))
+            ]
     core_rows = {}
 
     def forward(k):
@@ -134,8 +154,19 @@
 
     forward(0)
     down_copies = weight_copies(2)
+    if relay:
+        rows_in[3] = []
     for k in range(1, share):
-        rows_in[k].wait_recv()
+        for copy in rows_in[k]:
+            copy.wait_recv()
+        if relay and k < 3:
+            part_k = (low, high)[k - 1]
+            rows_in[3].append(
+                go(send(
+                    arr.at[k, 0, part_k, :], arr.at[3, 0, part_k, :],
+                    b_s.at[share + k], b_r.at[share + k], share_peer(3 - k),
+                ))
+            )
         forward(k)
 
     for copy in (*own_w[:2],):
@@ -145,27 +176,11 @@
 
     core_sums = {}
     dp_sums = {}
+    relayed = {}
     rows = group * ROWS
-
-    def finish(k):
-        for m in range(1, group):
-            core_sums[k, m].wait_recv()
-
-        def add(at):
-            cols = pl.ds(at, 256)
-            total = part[k, 0, :, cols].astype(jnp.float32)
-            for m in range(1, group):
-                total = total + core_in[k, m, :, cols].astype(jnp.float32)
-            part[k, 0, :, cols] = total.astype(jnp.bfloat16)
-
-        tiles(width, 256, add)
-        if k:
-            dp_sums[k] = go(
-                send(part.at[k, 0], dp_in.at[k], d_s.at[k], d_r.at[k], share_peer(share - k))
-            )
-
-    order = [*range(1, share), 0]
-    for n, k in enumerate(order):
+    columns = [pl.ds(c * piece, piece) for c in range(PIECES)]
+
+    for k in range(share):
         for m in range(1, group):
             core_rows[k, m].wait_recv()
 
@@ -174,17 +189,53 @@
             x = arr[k].reshape(rows, width)
             gated = jnp.dot(x, wg[:, cols], preferred_element_type=jnp.float32)
             lifted = jnp.dot(x, wu[:, cols], preferred_element_type=jnp.float32)
-            hid[:, cols] = (gated / (1.0 + jnp.exp(-gated)) * lifted).astype(jnp.bfloat16)
+            hid[k, :, cols] = (gated / (1.0 + jnp.exp(-gated)) * lifted).astype(jnp.bfloat16)
 
         tiles(units, 256, first)
-        if n == 0:
-            own_w[2].wait()
-            for copy in down_copies:
-                copy.wait_recv()
+
+    own_w[2].wait()
+    for copy in down_copies:
+        copy.wait_recv()
+
+    def homeward(k, c):
+        cols = columns[c]
+        dp_sums[k, c] = go(
+            send(
+                part.at[k, 0, :, cols], dp_in.at[k, :, cols],
+                d_s.at[k, c], d_r.at[k, c], share_peer(back(k, share)),
+            )
+        )
+
+    def finish(k):
+        for m in range(1, group):
+            core_sums[k, m].wait_recv()
+        for c in range(PIECES):
+
+            def add(at, c=c):
+                cols = pl.ds(c * piece + at, 256)
+                total = part[k, 0, :, cols].astype(jnp.float32)
+                for m in range(1, group):
+                    total = total + core_in[k, m, :, cols].astype(jnp.float32)
+                part[k, 0, :, cols] = total.astype(jnp.bfloat16)
+
+            tiles(piece, 256, add)
+            if relay and k == 3:
+                for n, rows_n in enumerate((low, high)):
+                    relayed[n, c] = go(
+                        send(
+                            part.at[3, 0, rows_n, columns[c]], relay_in.at[n, :, columns[c]],
+                            r_s.at[n, c], r_r.at[n, c], share_peer(n + 1),
+                        )
+                    )
+            elif k and not relay:
+                homeward(k, c)
+
+    order = [3, 1, 2, 0] if relay else [*range(1, share), 0]
+    for n, k in enumerate(order):
 
         def second(at, k=k):
             cols = pl.ds(at, 256)
-            made = jnp.dot(hid[...], wd[:, cols], preferred_element_type=jnp.float32)
+            made = jnp.dot(hid[k], wd[:, cols], preferred_element_type=jnp.float32)
             part[k, :, :, cols] = made.astype(jnp.bfloat16).reshape(group, ROWS, 256)
 
         tiles(width, 256, second)
@@ -194,34 +245,53 @@
             )
         if n:
             finish(order[n - 1])
+
+    if relay:
+        for c in range(PIECES):
+            relayed[0, c].wait_recv()
+            relayed[1, c].wait_recv()
+
+            def add_relayed(at, c=c):
+                cols = pl.ds(c * piece + at, 256)
+                for n, rows_n in enumerate((low, high)):
+                    total = part[2 - n, 0, rows_n, cols].astype(jnp.float32)
+                    total = total + relay_in[n, :, cols].astype(jnp.float32)
+                    part[2 - n, 0, rows_n, cols] = total.astype(jnp.bfloat16)
+
+            tiles(piece, 256, add_relayed)
+            homeward(1, c)
+            homeward(2, c)
     finish(order[-1])
 
-    for k in range(1, share):
-        dp_sums[k].wait_recv()
-
-    def gather(at):
-        cols = pl.ds(at, 256)
-        total = part[0, 0, :, cols].astype(jnp.float32)
+    home = []
+    for c in range(PIECES):
         for k in range(1, share):
-            total = total + dp_in[k, :, cols].astype(jnp.float32)
-        wide[:, cols] = total
-
-    tiles(width, 256, gather)
-    home = []
-    for i in [*range(1, EXPERTS), 0]:
-        to = out if i == 0 else zout
-
-        def split(at, i=i, to=to):
-            cols = pl.ds(at, 256)
-            full = jnp.concatenate(
-                [wide[i * CAP : (i + 1) * CAP, cols], jnp.zeros((SLOTS - CAP, 256), jnp.float32)], 0
-            )
-            to[i, :, cols] = full.astype(jnp.bfloat16)
-
-        tiles(width, 256, split)
-        if i:
+            if (k, c) in dp_sums:
+                dp_sums[k, c].wait_recv()
+
+        def gather(at, c=c):
+            cols = pl.ds(c * piece + at, 256)
+            total = part[0, 0, :, cols].astype(jnp.float32)
+            for k in range(1, share):
+                if (k, c) in dp_sums:
+                    total = total + dp_in[k, :, cols].astype(jnp.float32)
+            wide[:, cols] = total
+            for i in range(EXPERTS):
+                full = jnp.concatenate(
+                    [wide[i * CAP : (i + 1) * CAP, cols], jnp.zeros((SLOTS - CAP, 256), jnp.float32)]
+                )
+                to = zout if i else out
+                to[i, :, cols] = full.astype(jnp.bfloat16)
+
+        tiles(piece, 256, gather)
+        for i in range(1, EXPERTS):
             home.append(
-                go(send(zout.at[i], out.at[i], o_s.at[i], o_r.at[i], z_peer(EXPERTS - i)))
+                go(
+                    send(
+                        zout.at[i, :, columns[c]], out.at[i, :, columns[c]],
+                        o_s.at[i, c], o_r.at[i, c], z_peer(EXPERTS - i),
+                    )
+                )
             )
     for copy in home:
         copy.wait_recv()
@@ -236,12 +306,12 @@
         block = ROWS * width * 2
         units = hidden // share
         held = (
-            block * (share * group * 2 + share * (group - 1) + share + 2)
+            block * (share * group * 3 + share + 3)
             + 3 * width * units * 2
-            + group * ROWS * units * 2
+            + share * group * ROWS * units * 2
             + 4 * EXPERTS * SLOTS * width * 2
         )
-        if held <= VMEM_LIMIT * 2 // 3:
+        if held <= VMEM_LIMIT * 7 // 8:
             return share
     return 1
 
@@ -266,20 +336,22 @@
             pltpu.VMEM((width, units), bf16),
             pltpu.VMEM((width, units), bf16),
             pltpu.VMEM((units, width), bf16),
-            pltpu.VMEM((group * ROWS, units), bf16),
+            pltpu.VMEM((share, group * ROWS, units), bf16),
             pltpu.VMEM((share, group, ROWS, width), bf16),
             pltpu.VMEM((share, group, ROWS, width), bf16),
             pltpu.VMEM((share, ROWS, width), bf16),
+            pltpu.VMEM((2, ROWS // 2, width), bf16),
             pltpu.VMEM((ROWS, width), jnp.float32),
             pltpu.VMEM((EXPERTS, SLOTS, width), bf16),
             *pairs(EXPERTS),
             *pairs(3, dp),
             dma((3,)),
-            *pairs(share),
+            *pairs(2 * share),
             *pairs(share, group),
             *pairs(share, group),
-            *pairs(share),
-            *pairs(EXPERTS),
+            *pairs(share, PIECES),
+            *pairs(2, PIECES),
+            *pairs(EXPERTS, PIECES),
             dma((1,)),
         ],
         compiler_params=pltpu.CompilerParams(

time: 249 us -> 194 us (0.78)
  Pallas kernels: 239 us -> 185 us
    pallas_call x1, Pallas kernels: 239 us -> 185 us  [experts(): pl.pallas_call(functools.partial(kernel, dp, share, group), out_shape=jax...]
where the time goes in v2:
time: 194 us
  Pallas kernels  185 us (95%)
  matrix products  5.71 us (3%)
  other arithmetic  2.97 us (2%)
    pallas_call x1, Pallas kernels, experts(): pl.pallas_call(functools.partial(kernel, dp, share, group), out_shape=jax...  185 us

profile of v2, /device:TPU:0, one launch (start us, length us, event | category | flops | bytes accessed | tf_op | source)
XLA Modules:
  0.0 194.1 jit_solution(8405594863448261165)
XLA Ops:
  0.0 0.7 broadcast_compare_fusion
  0.7 0.7 multiply_add_fusion
  1.4 0.2 convert_reduce_fusion
  1.6 1.4 fusion.2
  3.0 0.8 fusion.16
  3.8 2.9 %convolution_convert_fusion = bf16[320,2048]{1,0:T(8,128)(2,1)} fusion(bf16[192,2048]{1,0:T(8,128)(2,1)} %param.8, f32[2048]{0:T(1024)S(1)} %bitcast.7, f32[2048]{0:T(1024)S(1)} %bitcast.6, f32[192]{0:T(256)S(1)} %add_sqrt_fusion, pred[192]{0:T(512)(128)(4,1)S(1)} %broadcast_compare_fusion, s32[192]{0:T(256)S(1)} %fusion.14), kind=kOutput, calls=%fused_computation | convolution fusion | flops 254341120 | bytes 2115264 | tf_op jit(solution)/shard_map/ts,td->sd/dot_general | solution.py:385
  6.7 0.0 copy-start
  6.7 0.0 copy-start.1
  6.7 184.5 %shard_map.82 = bf16[4,80,2048]{2,1,0:T(8,128)(2,1)} custom-call(bf16[4,80,2048]{2,1,0:T(8,128)(2,1)} %bitcast.8, bf16[512,2048]{1,0:T(8,128)(2,1)} %gate.1, bf16[512,2048]{1,0:T(8,128)(2,1)} %up.1, bf16[2048,512]{1,0:T(8,128)(2,1)} %down.1), custom_call_target="tpu_custom_call" | custom-call | flops 14495514624 | bytes 25165824 | tf_op jit(solution)/shard_map/pallas_call | solution.py:328
  191.2 0.0 copy-done
  191.2 0.0 copy-done.1
  191.2 2.8 %fusion.1 = bf16[192,2048]{1,0:T(8,128)(2,1)} fusion(bf16[320,2048]{1,0:T(8,128)(2,1)} %bitcast.5, bf16[192,2048]{1,0:T(8,128)(2,1)S(1)} %copy-done, f32[192]{0:T(256)S(1)} %copy-done.1, s32[192]{0:T(256)S(1)} %fusion.14), kind=kOutput, calls=%fused_computation.3 | convolution fusion | flops 253292544 | bytes 2885120 | tf_op jit(solution)/shard_map/dot_general | solution.py:388
  (2 shorter events, 0.0 us)
Async XLA Ops:
  6.7 184.5 %copy-start = (bf16[192,2048]{1,0:T(8,128)(2,1)S(1)}, bf16[192,2048]{1,0:T(8,128)(2,1)}, u32[]{:S(2)}) copy-start(bf16[192,2048]{1,0:T(8,128)(2,1)} %param.8) | copy-start | bytes 2359300
  6.7 184.5 %copy-start.1 = (f32[192]{0:T(256)S(1)}, f32[192]{0:T(256)}, u32[]{:S(2)}) copy-start(f32[192]{0:T(256)} %param.11) | copy-start | bytes 2308
